TPU v7x, 512 devices: a whole 4x4x16 slice. The times are simulated.
512 devices in a mesh: rep: 64 (over y, z_hi, x, core), fsdp: 8 (over z_lo).
Axes of the slice: x: 4, y: 4, z: 16 (z_hi: 2, z_lo: 8; z = z_hi * 8 + z_lo), core: 2. Of those that a mesh axis runs over, the one named last changes fastest.
Arguments:
- local_weights: bfloat16 [64, 64, 6144], P('rep', 'fsdp'), may hold values from -16 to 16
- base_weights: float32 [64, 6144], P('fsdp'), may hold values from -6 to 6
- momentum: float32 [64, 6144], P('fsdp'), may hold values from -4 to 4
- scale_codes: int32 [64, 64, 48], P('rep', 'fsdp'), may hold values from 16 to 64
Outputs:
- new_base: float32 [64, 6144], P('fsdp')
- new_momentum: float32 [64, 6144], P('fsdp')
- full_fragment: bfloat16 [64, 6144], replicated
All inputs are finite; a program needn't handle non-finite values.
Results may differ from a plain program's by a relative error of at most 0.009.
Values may be sent and summed in bfloat16 or wider, within the bound.
A program may use at most 64 MiB of HBM per device.

v0:
```python
import jax
import jax.numpy as jnp
from jax import lax
from jax.sharding import PartitionSpec as P

outer_rate = 0.7
outer_mu = 0.9
clip_level = 4.0


def outer_update(average, base_rows, moment_rows):
    new_momentum = outer_mu * moment_rows + average
    new_base = base_rows - outer_rate * (average + outer_mu * new_momentum)
    return (new_base, new_momentum)


def local(local_weights, base_weights, momentum, scale_codes):
    local_rows = local_weights[0]
    code_rows = scale_codes[0]
    block_width = base_weights.shape[1] // code_rows.shape[1]
    scales = jnp.repeat(code_rows.astype(jnp.float32) / 64.0, block_width, axis=1)
    pseudo = base_weights - local_rows.astype(jnp.float32)
    quantized = jnp.clip(pseudo / scales, -clip_level, clip_level).astype(jnp.bfloat16)
    dequant = quantized.astype(jnp.float32) * scales
    replicas = lax.axis_size("rep")
    summed = lax.psum(dequant, "rep")
    new_base, new_momentum = outer_update(summed / replicas, base_weights, momentum)
    full_fragment = lax.all_gather(new_base.astype(jnp.bfloat16), "fsdp", axis=0, tiled=True)
    return (new_base, new_momentum, full_fragment)


def solution(mesh):
    in_specs = (P("rep", "fsdp", None), P("fsdp", None), P("fsdp", None), P("rep", "fsdp", None))
    out_specs = (P("fsdp", None), P("fsdp", None), P())
    return jax.shard_map(local, mesh=mesh, in_specs=in_specs, out_specs=out_specs, check_vma=False)
```

profile of v0, /device:TPU:1, one launch (start us, length us, event | category | flops | bytes accessed | tf_op | source)
XLA Modules:
  0.0 1088.8 jit_solution(17723581233006442930)
XLA Ops:
  7.2 0.0 all-reduce.2.cloned.1.call-start
  7.2 0.7 multiply_bitcast_fusion
  7.9 0.1 copy.7
  8.0 0.0 copy-start.1
  8.0 1.8 bitcast_multiply_fusion
  9.8 0.0 copy-start
  9.8 0.0 all-reduce.2.cloned.1.call-update
  9.8 1027.4 %all-reduce.2.cloned.1.call-done = f32[8,6144]{1,0:T(8,128)} async-done(((f32[8,6144]{1,0:T(8,128)}), f32[8,6144]{1,0:T(8,128)}) %all-reduce.2.cloned.1.call-update) | async-done | bytes 196624 | tf_op jit(solution)/shard_map/psum | solution.py:26
  1037.2 0.0 copy-done.1
  1037.2 0.0 copy-done
  1037.2 1.7 fusion.2
  1039.0 42.1 %all_gather.3 = bf16[64,6144]{1,0:T(8,128)(2,1)S(1)} all-gather(bf16[8,6144]{1,0:T(8,128)(2,1)S(1)} %get-tuple-element.3), channel_id=1, replica_groups=mesh['rep'=64,'fsdp'=8] {'fsdp'}, dimensions={0}, use_global_device_ids=true | all-gather | bytes 884736 | tf_op jit(solution)/shard_map/all_gather | solution.py:28
  1081.0 0.9 copy.10
Async XLA Ops:
  7.2 1030.1 %all-reduce.2.cloned.1.call-start = ((), (), s32[]{:S(2)}) async-start(), calls=%async_computation | async-start | bytes 393216 | tf_op jit(solution)/shard_map/psum | solution.py:26
  8.0 1029.2 %copy-start.1 = (f32[8,6144]{1,0:T(8,128)S(1)}, f32[8,6144]{1,0:T(8,128)}, u32[]{:S(2)}) copy-start(f32[8,6144]{1,0:T(8,128)} %param.6) | copy-start | bytes 589828
  9.8 1027.4 %copy-start = (f32[8,6144]{1,0:T(8,128)S(1)}, f32[8,6144]{1,0:T(8,128)}, u32[]{:S(2)}) copy-start(f32[8,6144]{1,0:T(8,128)} %param.5) | copy-start | bytes 589828
Sparse Core Ops, SparseCore 0:
  11.5 1025.7 all-reduce.1
where the time goes:
time: 1100 us; the launch traced here: 1090 us
  waiting for transfers between devices  1030 us (94%)
  blocking collectives  42.1 us (4%)
  between operations  14 us (1%)
    psum x1, waiting for transfers between devices, local(): summed = lax.psum(dequant, 'rep')  1030 us
    all_gather x1, blocking collectives, local(): lax.all_gather(new_base.astype(jnp.bfloat16), 'fsdp', axis=0, tiled=True)  42.1 us
  transfers between devices with their start and end apart: 1, of which 1 were waited for; matrix products, arithmetic and copies ran while one was open for 0% of the time, Pallas kernels for 0%

commit v1 on v0

v1 whole, which is shorter than its diff:
```python
import jax
import jax.numpy as jnp
from jax import lax
from jax.experimental import pallas as pl
from jax.experimental.pallas import tpu as pltpu
from jax.sharding import PartitionSpec as P

outer_rate = 0.7
outer_mu = 0.9
clip_level = 4.0

ROWS = 8
COLS = 6144
LANES = 128
UNIT = 256
UNITS = COLS // UNIT
PLANE = 32
Z = 16
FSDP = 8
REPLICAS = 64
MESH = pl.DeviceIdType.MESH

OFFSETS = sorted(
    [(dx, dy) for dy in range(4) for dx in range(4)],
    key=lambda o: -(min(o[0], 4 - o[0]) + min(o[1], 4 - o[1])),
)


def kernel(local_hbm, base_hbm, moment_hbm, codes_hbm, new_base_ref, new_moment_ref, full_ref,
           local, base, moment, codes, terms, arrived, partials, us, rows,
           load_sem, term_send, term_recv, u_send, u_recv, part_send, part_recv, row_send, sib_send, row_recv, out_sem):
    rep = lax.axis_index("rep")
    zl = lax.axis_index("fsdp")
    c = rep % 2
    x = (rep // 2) % 4
    zh = (rep // 8) % 2
    y = rep // 16
    z = zh * FSDP + zl
    even = (x + y) % 2 == 0
    owner = jnp.logical_or(c == 0, even)
    my_unit = jnp.where(c == 0, y * 4 + x, 16 + y * 2 + x // 2)
    xs = [(x + d) % 4 for d in range(4)]
    ys = [(y + d) % 4 for d in range(4)]

    def in_plane(px, py, pc):
        return (py * 16 + zh * 8 + px * 2 + pc, zl)

    def along_z(d):
        zt = (z + d + Z) % Z
        return (y * 16 + (zt // FSDP) * 8 + x * 2 + c, zt % FSDP)

    loads = [
        pltpu.make_async_copy(src, dst, load_sem.at[i])
        for i, (src, dst) in enumerate(((codes_hbm, codes), (local_hbm, local), (base_hbm, base), (moment_hbm, moment)))
    ]
    for load in loads:
        load.start()

    barrier = pltpu.get_barrier_semaphore()
    z_near = (4, -4, 3, -3, 2, -2, 1, -1)
    for d in z_near:
        pl.semaphore_signal(barrier, inc=1, device_id=along_z(d), device_id_type=MESH)
    for dx, dy in OFFSETS:
        for pc in (c, 1 - c) if (dx, dy) != (0, 0) else (1 - c,):
            pl.semaphore_signal(barrier, inc=1, device_id=in_plane(xs[dx], ys[dy], pc), device_id_type=MESH)

    for load in loads:
        load.wait()

    scales = codes[0].astype(jnp.float32) / 64.0
    inverse = 1.0 / scales

    def term(j):
        cols = slice(j * LANES, (j + 1) * LANES)
        pseudo = base[:, cols] - local[0, :, cols].astype(jnp.float32)
        quantized = jnp.clip(pseudo * inverse[:, j:j + 1], -clip_level, clip_level).astype(jnp.bfloat16)
        return quantized.astype(jnp.float32) * scales[:, j:j + 1]

    for unit in range(UNITS):
        terms[unit] = jnp.concatenate([term(2 * unit), term(2 * unit + 1)], axis=0).astype(jnp.bfloat16)

    halves = []
    for half in range(2):
        cols = pl.ds(pl.multiple_of(my_unit * UNIT + half * LANES, LANES), LANES)
        halves.append(base[:, cols] - (outer_rate * outer_mu * outer_mu) * moment[:, cols])

    @pl.when(owner)
    def _():
        us[zl] = jnp.concatenate(halves, axis=0)

    pl.semaphore_wait(barrier, len(z_near) + PLANE - 1)

    def send_term(px, py, pc, to_core):
        unit = py * 4 + px if to_core == 0 else 16 + py * 2 + px // 2
        slot = (((py - y + 4) % 4) * 4 + (px - x + 4) % 4) * 2 + (c if to_core == 0 else 1 - c) - 1
        pltpu.make_async_remote_copy(
            src_ref=terms.at[unit], dst_ref=arrived.at[slot], send_sem=term_send, recv_sem=term_recv,
            device_id=in_plane(px, py, pc), device_id_type=MESH,
        ).start()

    second = [(dx2, dy) for dy in (2, 1, 3, 0) for dx2 in (1, 0)]
    for i, (dx, dy) in enumerate(OFFSETS):
        if (dx, dy) == (0, 0):
            @pl.when(c == 1)
            def _():
                send_term(x, y, 0, 0)
        else:
            send_term(xs[dx], ys[dy], 0, 0)
        if i % 2 == 1:
            dx2, sy = second[i // 2]
            px = ys[sy] % 2 + 2 * ((x // 2 + dx2) % 2)
            if (dx2, sy) == (0, 0):
                @pl.when(jnp.logical_not(jnp.logical_and(c == 1, even)))
                def _():
                    send_term(px, ys[sy], 1, 1)
            else:
                send_term(px, ys[sy], 1, 1)

    def send(src, dst, send_sem, recv_sem, to):
        return pltpu.make_async_remote_copy(
            src_ref=src, dst_ref=dst, send_sem=send_sem, recv_sem=recv_sem, device_id=to, device_id_type=MESH)

    @pl.when(owner)
    def _():
        for d in (4, 3, -3, 2, -2, 1, -1):
            send(us.at[zl], us.at[zl], u_send, u_recv, along_z(d)).start()

        pltpu.make_async_copy(arrived, arrived, term_recv).wait()
        total = terms[my_unit].astype(jnp.float32)
        for slot in range(PLANE - 1):
            total += arrived[slot].astype(jnp.float32)
        partials[z] = total.astype(jnp.bfloat16)
        pltpu.make_async_copy(us.at[0:FSDP - 1], us.at[0:FSDP - 1], u_recv).wait()

        for d in (8, 7, -7, 6, -6, 5, -5, 4, -4, 3, -3, 2, -2, 1, -1):
            send(partials.at[z], partials.at[z], part_send, part_recv, along_z(d)).start()
        pltpu.make_async_copy(partials.at[0:Z - 1], partials.at[0:Z - 1], part_recv).wait()

        def summed(f):
            return partials[f].astype(jnp.float32) + partials[f + FSDP].astype(jnp.float32)

        updated = [us[f] - (outer_rate * (1.0 + outer_mu) / REPLICAS) * summed(f) for f in range(FSDP)]
        mine = summed(zl)
        high = mine.astype(jnp.bfloat16).astype(jnp.float32)
        low = mine - high
        for half in range(2):
            cols = pl.ds(pl.multiple_of(my_unit * UNIT + half * LANES, LANES), LANES)
            part = slice(half * ROWS, (half + 1) * ROWS)
            for g in range(FSDP // 2):
                pair = jnp.concatenate([updated[2 * g][part], updated[2 * g + 1][part]], axis=0)
                rows[16 * g:16 * g + 16, cols] = pair.astype(jnp.bfloat16)
            rows[64:80, cols] = jnp.concatenate([high[part], low[part]], axis=0).astype(jnp.bfloat16)

        block = rows.at[:, pl.ds(pl.multiple_of(my_unit * UNIT, UNIT), UNIT)]
        for dx, dy in OFFSETS:
            if (dx, dy) != (0, 0):
                send(block, block, row_send, row_recv, in_plane(xs[dx], ys[dy], c)).start()
            send(block, block, sib_send, row_recv, in_plane(xs[dx], ys[dy], 1 - c)).start()
        others = rows.at[:, 0:(UNITS - 1) * UNIT]
        pltpu.make_async_copy(others, others, row_recv).wait()

    @pl.when(jnp.logical_not(owner))
    def _():
        pltpu.make_async_copy(rows, rows, row_recv).wait()

    full_copy = pltpu.make_async_copy(rows.at[0:64], full_ref, out_sem)
    full_copy.start()
    for j in range(COLS // LANES):
        cols = slice(j * LANES, (j + 1) * LANES)
        split = rows[64:80, cols].astype(jnp.float32)
        average = (split[0:ROWS] + split[ROWS:2 * ROWS]) / REPLICAS
        new_moment = outer_mu * moment[:, cols] + average
        new_moment_ref[:, cols] = new_moment
        new_base_ref[:, cols] = base[:, cols] - outer_rate * (average + outer_mu * new_moment)
    full_copy.wait()

    @pl.when(owner)
    def _():
        own = terms.at[0:UNITS - 1]
        pltpu.make_async_copy(own, own, term_send).wait()
        pltpu.make_async_copy(us.at[0:FSDP - 1], us.at[0:FSDP - 1], u_send).wait()
        pltpu.make_async_copy(partials.at[0:Z - 1], partials.at[0:Z - 1], part_send).wait()
        sent = rows.at[:, 0:15 * UNIT]
        pltpu.make_async_copy(sent, sent, row_send).wait()
        sent = rows.at[:, 0:16 * UNIT]
        pltpu.make_async_copy(sent, sent, sib_send).wait()

    @pl.when(jnp.logical_not(owner))
    def _():
        pltpu.make_async_copy(terms, terms, term_send).wait()


def step(local_weights, base_weights, momentum, scale_codes):
    anywhere = pl.BlockSpec(memory_space=pl.ANY)
    vmem = pl.BlockSpec(memory_space=pltpu.VMEM)
    dma = pltpu.SemaphoreType.DMA
    return pl.pallas_call(
        kernel,
        out_shape=(
            jax.ShapeDtypeStruct((ROWS, COLS), jnp.float32),
            jax.ShapeDtypeStruct((ROWS, COLS), jnp.float32),
            jax.ShapeDtypeStruct((FSDP * ROWS, COLS), jnp.bfloat16),
        ),
        in_specs=[anywhere] * 4,
        out_specs=(vmem, vmem, anywhere),
        scratch_shapes=[
            pltpu.VMEM((1, ROWS, COLS), jnp.bfloat16),
            pltpu.VMEM((ROWS, COLS), jnp.float32),
            pltpu.VMEM((ROWS, COLS), jnp.float32),
            pltpu.VMEM((1, ROWS, COLS // LANES), jnp.int32),
            pltpu.VMEM((UNITS, 16, LANES), jnp.bfloat16),
            pltpu.VMEM((PLANE - 1, 16, LANES), jnp.bfloat16),
            pltpu.VMEM((Z, 16, LANES), jnp.bfloat16),
            pltpu.VMEM((FSDP, 16, LANES), jnp.float32),
            pltpu.VMEM((80, COLS), jnp.bfloat16),
            dma((4,)), dma, dma, dma, dma, dma, dma, dma, dma, dma, dma,
        ],
        compiler_params=pltpu.CompilerParams(collective_id=0, has_side_effects=True, vmem_limit_bytes=16 * 1024 * 1024),
        name="outer_step",
    )(local_weights, base_weights, momentum, scale_codes)


def solution(mesh):
    in_specs = (P("rep", "fsdp", None), P("fsdp", None), P("fsdp", None), P("rep", "fsdp", None))
    out_specs = (P("fsdp", None), P("fsdp", None), P())
    return jax.shard_map(step, mesh=mesh, in_specs=in_specs, out_specs=out_specs, check_vma=False)
```

time: 1100 us -> 48.7 us (0.04); the launches traced: 1090 us -> 48.5 us
  waiting for transfers between devices: 1030 us -> 0 us
  Pallas kernels: 0 us -> 42.1 us
  blocking collectives: 42.1 us -> 0 us
  between operations: 14 us -> 0.65 us
    psum x1 -> x0, waiting for transfers between devices: 1030 us -> none  [local(): summed = lax.psum(dequant, 'rep')]
    pallas_call x0 -> x1, Pallas kernels: none -> 42.1 us  [step(): pl.pallas_call(kernel, out_shape=(jax.ShapeDtypeStruct((ROWS, COLS), jnp....]
    all_gather x1 -> x0, blocking collectives: 42.1 us -> none  [local(): lax.all_gather(new_base.astype(jnp.bfloat16), 'fsdp', axis=0, tiled=True)]
  transfers between devices with their start and end apart: 1 -> 0, of which waited for: 1 -> 0; matrix products, arithmetic and copies ran while one was open for 0% -> 0% of each run, Pallas kernels for 0% -> 0%
where the time goes in v1:
time: 48.7 us; the launch traced here: 48.5 us
  Pallas kernels  42.1 us (86%)
  local copies, waits for them, and re-layouts  5.66 us (12%)
  between operations  0.65 us (1%)
    pallas_call x1, Pallas kernels, step(): pl.pallas_call(kernel, out_shape=(jax.ShapeDtypeStruct((ROWS, COLS), jnp....  42.1 us
    unnamed x11, local copies, waits for them, and re-layouts  5.66 us

profile of v1, /device:TPU:1, one launch (start us, length us, event | category | flops | bytes accessed | tf_op | source)
XLA Modules:
  0.0 48.5 jit_solution(14572292720929421562)
XLA Ops:
  0.6 0.0 copy-start
  0.6 0.9 %copy-done = f32[8,6144]{1,0:T(8,128)S(1)} copy-done((f32[8,6144]{1,0:T(8,128)S(1)}, f32[8,6144]{1,0:T(8,128)}, u32[]{:S(2)}) %copy-start) | copy-done | bytes 196632
  1.6 0.0 copy-start.1
  1.6 0.9 %copy-done.1 = f32[8,6144]{1,0:T(8,128)S(1)} copy-done((f32[8,6144]{1,0:T(8,128)S(1)}, f32[8,6144]{1,0:T(8,128)}, u32[]{:S(2)}) %copy-start.1) | copy-done | bytes 196632
  2.5 0.0 copy-start.2
  2.5 0.9 %copy-done.2 = bf16[1,8,6144]{2,1,0:T(8,128)(2,1)S(1)} copy-done((bf16[1,8,6144]{2,1,0:T(8,128)(2,1)S(1)}, bf16[1,8,6144]{2,1,0:T(8,128)(2,1)}, u32[]{:S(2)}) %copy-start.2) | copy-done | bytes 98328
  3.4 0.0 copy-start.3
  3.4 0.7 %copy-done.3 = s32[1,8,48]{2,1,0:T(8,128)S(1)} copy-done((s32[1,8,48]{2,1,0:T(8,128)S(1)}, s32[1,8,48]{2,1,0:T(8,128)}, u32[]{:S(2)}) %copy-start.3) | copy-done | bytes 1560
  4.1 42.1 %outer_step.1 = (f32[8,6144]{1,0:T(8,128)S(1)}, f32[8,6144]{1,0:T(8,128)S(1)}, bf16[64,6144]{1,0:T(8,128)(2,1)S(1)}) custom-call(bf16[1,8,6144]{2,1,0:T(8,128)(2,1)S(1)} %copy-done.2, f32[8,6144]{1,0:T(8,128)S(1)} %copy-done, f32[8,6144]{1,0:T(8,128)S(1)} %copy-done.1, s32[1,8,48]{2,1,0:T(8,128)S(1)} %copy-done.3), custom_call_target="tpu_custom_call" | custom-call | tf_op jit(solution)/shard_map/outer_step/pallas_call | solution.py:197
  46.2 0.7 %copy.10 = f32[8,6144]{1,0:T(8,128)} copy(f32[8,6144]{1,0:T(8,128)S(1)} %get-tuple-element.6) | data formatting | bytes 393216
  46.9 0.7 %copy.11 = f32[8,6144]{1,0:T(8,128)} copy(f32[8,6144]{1,0:T(8,128)S(1)} %get-tuple-element.7) | data formatting | bytes 393216
  47.6 0.9 %copy.12 = bf16[64,6144]{1,0:T(8,128)(2,1)} copy(bf16[64,6144]{1,0:T(8,128)(2,1)S(1)} %get-tuple-element.8) | data formatting | bytes 1572864
Async XLA Ops:
  0.6 0.9 %copy-start = (f32[8,6144]{1,0:T(8,128)S(1)}, f32[8,6144]{1,0:T(8,128)}, u32[]{:S(2)}) copy-start(f32[8,6144]{1,0:T(8,128)} %base_hbm.1) | copy-start | bytes 589828
  1.6 0.9 %copy-start.1 = (f32[8,6144]{1,0:T(8,128)S(1)}, f32[8,6144]{1,0:T(8,128)}, u32[]{:S(2)}) copy-start(f32[8,6144]{1,0:T(8,128)} %moment_hbm.1) | copy-start | bytes 589828
  2.5 0.9 %copy-start.2 = (bf16[1,8,6144]{2,1,0:T(8,128)(2,1)S(1)}, bf16[1,8,6144]{2,1,0:T(8,128)(2,1)}, u32[]{:S(2)}) copy-start(bf16[1,8,6144]{2,1,0:T(8,128)(2,1)} %local_hbm.1) | copy-start | bytes 294916
  3.4 0.7 %copy-start.3 = (s32[1,8,48]{2,1,0:T(8,128)S(1)}, s32[1,8,48]{2,1,0:T(8,128)}, u32[]{:S(2)}) copy-start(s32[1,8,48]{2,1,0:T(8,128)} %codes_hbm.1) | copy-start | bytes 4612

commit v2 on v1

--- a/solution.py
+++ b/solution.py
@@ -26,9 +26,9 @@
 )
 
 
-def kernel(local_hbm, base_hbm, moment_hbm, codes_hbm, new_base_ref, new_moment_ref, full_ref,
-           local, base, moment, codes, terms, arrived, partials, us, rows,
-           load_sem, term_send, term_recv, u_send, u_recv, part_send, part_recv, row_send, sib_send, row_recv, out_sem):
+def kernel(local_hbm, base_hbm, moment_hbm, codes_hbm, new_base_ref, new_moment_ref, rows,
+           local, base, moment, codes, terms, arrived, partials, us,
+           load_sem, term_send, term_recv, u_send, u_recv, part_send, part_recv, row_send, sib_send, row_recv):
     rep = lax.axis_index("rep")
     zl = lax.axis_index("fsdp")
     c = rep % 2
@@ -163,8 +163,6 @@
     def _():
         pltpu.make_async_copy(rows, rows, row_recv).wait()
 
-    full_copy = pltpu.make_async_copy(rows.at[0:64], full_ref, out_sem)
-    full_copy.start()
     for j in range(COLS // LANES):
         cols = slice(j * LANES, (j + 1) * LANES)
         split = rows[64:80, cols].astype(jnp.float32)
@@ -172,7 +170,6 @@
         new_moment = outer_mu * moment[:, cols] + average
         new_moment_ref[:, cols] = new_moment
         new_base_ref[:, cols] = base[:, cols] - outer_rate * (average + outer_mu * new_moment)
-    full_copy.wait()
 
     @pl.when(owner)
     def _():
@@ -190,34 +187,56 @@
         pltpu.make_async_copy(terms, terms, term_send).wait()
 
 
+def finish(new_base, new_moment, rows, new_base_out, new_moment_out, full_out, sems):
+    copies = [
+        pltpu.make_async_copy(src, dst, sems.at[i])
+        for i, (src, dst) in enumerate(((rows.at[0:64], full_out), (new_base, new_base_out), (new_moment, new_moment_out)))
+    ]
+    for copy in copies:
+        copy.start()
+    for copy in copies:
+        copy.wait()
+
+
 def step(local_weights, base_weights, momentum, scale_codes):
     anywhere = pl.BlockSpec(memory_space=pl.ANY)
     vmem = pl.BlockSpec(memory_space=pltpu.VMEM)
     dma = pltpu.SemaphoreType.DMA
+    results = pl.pallas_call(
+        kernel,
+        out_shape=(
+            pltpu.VMEM((ROWS, COLS), jnp.float32),
+            pltpu.VMEM((ROWS, COLS), jnp.float32),
+            pltpu.VMEM((80, COLS), jnp.bfloat16),
+        ),
+        in_specs=[pl.BlockSpec(memory_space=pltpu.HBM)] * 4,
+        out_specs=(vmem, vmem, vmem),
+        scratch_shapes=[
+            pltpu.VMEM((1, ROWS, COLS), jnp.bfloat16),
+            pltpu.VMEM((ROWS, COLS), jnp.float32),
+            pltpu.VMEM((ROWS, COLS), jnp.float32),
+            pltpu.VMEM((1, ROWS, COLS // LANES), jnp.int32),
+            pltpu.VMEM((UNITS, 16, LANES), jnp.bfloat16),
+            pltpu.VMEM((PLANE - 1, 16, LANES), jnp.bfloat16),
+            pltpu.VMEM((Z, 16, LANES), jnp.bfloat16),
+            pltpu.VMEM((FSDP, 16, LANES), jnp.float32),
+            dma((4,)), dma, dma, dma, dma, dma, dma, dma, dma, dma,
+        ],
+        compiler_params=pltpu.CompilerParams(collective_id=0, has_side_effects=True, vmem_limit_bytes=60 * 1024 * 1024),
+        name="outer_step",
+    )(local_weights, base_weights, momentum, scale_codes)
     return pl.pallas_call(
-        kernel,
+        finish,
         out_shape=(
             jax.ShapeDtypeStruct((ROWS, COLS), jnp.float32),
             jax.ShapeDtypeStruct((ROWS, COLS), jnp.float32),
             jax.ShapeDtypeStruct((FSDP * ROWS, COLS), jnp.bfloat16),
         ),
-        in_specs=[anywhere] * 4,
-        out_specs=(vmem, vmem, anywhere),
-        scratch_shapes=[
-            pltpu.VMEM((1, ROWS, COLS), jnp.bfloat16),
-            pltpu.VMEM((ROWS, COLS), jnp.float32),
-            pltpu.VMEM((ROWS, COLS), jnp.float32),
-            pltpu.VMEM((1, ROWS, COLS // LANES), jnp.int32),
-            pltpu.VMEM((UNITS, 16, LANES), jnp.bfloat16),
-            pltpu.VMEM((PLANE - 1, 16, LANES), jnp.bfloat16),
-            pltpu.VMEM((Z, 16, LANES), jnp.bfloat16),
-            pltpu.VMEM((FSDP, 16, LANES), jnp.float32),
-            pltpu.VMEM((80, COLS), jnp.bfloat16),
-            dma((4,)), dma, dma, dma, dma, dma, dma, dma, dma, dma, dma,
-        ],
-        compiler_params=pltpu.CompilerParams(collective_id=0, has_side_effects=True, vmem_limit_bytes=16 * 1024 * 1024),
-        name="outer_step",
-    )(local_weights, base_weights, momentum, scale_codes)
+        in_specs=[vmem] * 3,
+        out_specs=(anywhere,) * 3,
+        scratch_shapes=[dma((3,))],
+        name="write_out",
+    )(*results)
 
 
 def solution(mesh):

time: 48.7 us -> 47 us (0.965)
  local copies, waits for them, and re-layouts: 5.66 us -> 2.31 us
  Pallas kernels: 42.1 us -> 43.9 us
    unnamed x11 -> x6, local copies, waits for them, and re-layouts: 5.66 us -> 2.31 us
    pallas_call x1 -> x2, Pallas kernels: 42.1 us -> 43.9 us  [the longest x1 41.5 us: step(): pl.pallas_call(kernel, out_shape=(pltpu.VMEM((ROWS, COLS), jnp.float32),...]
where the time goes in v2:
time: 47 us; the launch traced here: 46.8 us
  Pallas kernels  43.9 us (93%)
  local copies, waits for them, and re-layouts  2.31 us (5%)
  between operations  0.65 us (1%)
    pallas_call x1, Pallas kernels, step(): pl.pallas_call(kernel, out_shape=(pltpu.VMEM((ROWS, COLS), jnp.float32),...  41.5 us
    pallas_call x1, Pallas kernels, step(): pl.pallas_call(finish, out_shape=(jax.ShapeDtypeStruct((ROWS, COLS), jnp....  2.43 us
    unnamed x6, local copies, waits for them, and re-layouts  2.31 us

profile of v2, /device:TPU:1, one launch (start us, length us, event | category | flops | bytes accessed | tf_op | source)
XLA Modules:
  0.0 46.8 jit_solution(16264905419355658023)
XLA Ops:
  0.6 41.5 %outer_step.1 = (f32[8,6144]{1,0:T(8,128)S(1)}, f32[8,6144]{1,0:T(8,128)S(1)}, bf16[80,6144]{1,0:T(8,128)(2,1)S(1)}) custom-call(bf16[1,8,6144]{2,1,0:T(8,128)(2,1)} %local_hbm.1, f32[8,6144]{1,0:T(8,128)} %base_hbm.1, f32[8,6144]{1,0:T(8,128)} %moment_hbm.1, s32[1,8,48]{2,1,0:T(8,128)} %codes_hbm.1), custom_call_target="tpu_custom_call" | custom-call | tf_op jit(solution)/shard_map/outer_step/pallas_call | solution.py:205
  42.1 0.0 copy-start
  42.1 1.0 %copy-done = bf16[80,6144]{1,0:T(8,128)(2,1)} copy-done((bf16[80,6144]{1,0:T(8,128)(2,1)}, bf16[80,6144]{1,0:T(8,128)(2,1)S(1)}, u32[]{:S(2)}) %copy-start) | copy-done | bytes 983064
  43.1 0.0 copy-start.1
  43.1 0.7 %copy-done.1 = f32[8,6144]{1,0:T(8,128)} copy-done((f32[8,6144]{1,0:T(8,128)}, f32[8,6144]{1,0:T(8,128)S(1)}, u32[]{:S(2)}) %copy-start.1) | copy-done | bytes 196632
  43.7 0.0 copy-start.2
  43.7 0.7 %copy-done.2 = f32[8,6144]{1,0:T(8,128)} copy-done((f32[8,6144]{1,0:T(8,128)}, f32[8,6144]{1,0:T(8,128)S(1)}, u32[]{:S(2)}) %copy-start.2) | copy-done | bytes 196632
  44.4 2.4 %write_out.1 = (f32[8,6144]{1,0:T(8,128)}, f32[8,6144]{1,0:T(8,128)}, bf16[64,6144]{1,0:T(8,128)(2,1)}) custom-call(f32[8,6144]{1,0:T(8,128)} %copy-done.1, f32[8,6144]{1,0:T(8,128)} %copy-done.2, bf16[80,6144]{1,0:T(8,128)(2,1)} %copy-done), custom_call_target="tpu_custom_call" | custom-call | tf_op jit(solution)/shard_map/write_out/pallas_call | solution.py:228
Async XLA Ops:
  42.1 1.0 %copy-start = (bf16[80,6144]{1,0:T(8,128)(2,1)}, bf16[80,6144]{1,0:T(8,128)(2,1)S(1)}, u32[]{:S(2)}) copy-start(bf16[80,6144]{1,0:T(8,128)(2,1)S(1)} %get-tuple-element.8.rows) | copy-start | bytes 2949124
  43.1 0.7 %copy-start.1 = (f32[8,6144]{1,0:T(8,128)}, f32[8,6144]{1,0:T(8,128)S(1)}, u32[]{:S(2)}) copy-start(f32[8,6144]{1,0:T(8,128)S(1)} %get-tuple-element.6.new_base) | copy-start | bytes 589828
  43.7 0.7 %copy-start.2 = (f32[8,6144]{1,0:T(8,128)}, f32[8,6144]{1,0:T(8,128)S(1)}, u32[]{:S(2)}) copy-start(f32[8,6144]{1,0:T(8,128)S(1)} %get-tuple-element.7.new_moment) | copy-start | bytes 589828

commit v3 on v2

v3 whole, which is shorter than its diff:
```python
import jax
import jax.numpy as jnp
from jax import lax
from jax.experimental import pallas as pl
from jax.experimental.pallas import tpu as pltpu
from jax.sharding import PartitionSpec as P

outer_rate = 0.7
outer_mu = 0.9
clip_level = 4.0

ROWS = 8
COLS = 6144
LANES = 128
CHIPS = 16
SPAN = COLS // CHIPS
Z = 16
FSDP = 8
REPLICAS = 64
MESH = pl.DeviceIdType.MESH

OFFSETS = sorted(
    [(dx, dy) for dy in range(4) for dx in range(4)],
    key=lambda o: -(min(o[0], 4 - o[0]) + min(o[1], 4 - o[1])),
)


def wait_bytes(ref, sem):
    pltpu.make_async_copy(ref, ref, sem).wait()


def kernel(local_hbm, base_hbm, moment_hbm, codes_hbm, new_base_ref, new_moment_ref, rows,
           local, base, moment, codes, terms0, terms1, arrived0, arrived1, mine0, mine1, parts0, parts1, us,
           load_sem, term_send, term_recv, u_send, u_recv, part_send, part_recv, row_send, row_recv, pass_send, pass_recv):
    rep = lax.axis_index("rep")
    zl = lax.axis_index("fsdp")
    c = rep % 2
    x = (rep // 2) % 4
    zh = (rep // 8) % 2
    y = rep // 16
    z = zh * FSDP + zl
    half = zl // 4
    home = (zl // 2) % 2
    at_home = c == home
    first = (y * 4 + x) * SPAN
    xs = [(x + d) % 4 for d in range(4)]
    ys = [(y + d) % 4 for d in range(4)]

    def in_plane(dx, dy, pc):
        return (ys[dy] * 16 + zh * 8 + xs[dx] * 2 + pc, zl)

    def along_z(d, pc):
        zt = (z + d + Z) % Z
        return (y * 16 + (zt // FSDP) * 8 + x * 2 + pc, zt % FSDP)

    def send(src, dst, send_sem, recv_sem, to):
        pltpu.make_async_remote_copy(
            src_ref=src, dst_ref=dst, send_sem=send_sem, recv_sem=recv_sem, device_id=to, device_id_type=MESH).start()

    loads = [
        pltpu.make_async_copy(src, dst, load_sem.at[i])
        for i, (src, dst) in enumerate(((codes_hbm, codes), (local_hbm, local), (base_hbm, base), (moment_hbm, moment)))
    ]
    for load in loads:
        load.start()

    barrier = pltpu.get_barrier_semaphore()
    for dx, dy in OFFSETS:
        for pc in (c, 1 - c) if (dx, dy) != (0, 0) else (1 - c,):
            pl.semaphore_signal(barrier, inc=1, device_id=in_plane(dx, dy, pc), device_id_type=MESH)
    z_near = (4, -4, 3, -3, 2, -2, 1, -1)
    for d in z_near:
        for pc in (c, 1 - c):
            pl.semaphore_signal(barrier, inc=1, device_id=along_z(d, pc), device_id_type=MESH)

    for load in loads:
        load.wait()

    scales = codes[0].astype(jnp.float32) / 64.0
    inverse = 1.0 / scales

    def term(j):
        cols = slice(j * LANES, (j + 1) * LANES)
        pseudo = base[:, cols] - local[0, :, cols].astype(jnp.float32)
        quantized = jnp.clip(pseudo * inverse[:, j:j + 1], -clip_level, clip_level).astype(jnp.bfloat16)
        return quantized.astype(jnp.float32) * scales[:, j:j + 1]

    for k in range(CHIPS):
        terms0[k] = jnp.concatenate([term(3 * k), term(3 * k + 1)], axis=0).astype(jnp.bfloat16)
        terms1[k] = term(3 * k + 2)

    for j in range(3):
        cols = pl.ds(pl.multiple_of(first + j * LANES, LANES), LANES)
        us[zl, j] = base[:, cols] - (outer_rate * outer_mu * outer_mu) * moment[:, cols]

    pl.semaphore_wait(barrier, 2 * len(z_near) + 2 * CHIPS - 1)

    for dx, dy in OFFSETS:
        k = ys[dy] * 4 + xs[dx]
        slot = (dy * 4 + dx) * 2 - 1
        if (dx, dy) == (0, 0):
            @pl.when(c == 1)
            def _():
                send(terms0.at[k], arrived0.at[0], term_send, term_recv, in_plane(0, 0, 0))

            @pl.when(c == 0)
            def _():
                send(terms1.at[k], arrived1.at[0], term_send, term_recv, in_plane(0, 0, 1))
        else:
            send(terms0.at[k], arrived0.at[slot + c], term_send, term_recv, in_plane(dx, dy, 0))
            send(terms1.at[k], arrived1.at[slot + 1 - c], term_send, term_recv, in_plane(dx, dy, 1))
    for d in (4, 3, -3, 2, -2, 1, -1):
        send(us.at[zl], us.at[zl], u_send, u_recv, along_z(d, c))

    wait_bytes(arrived0, term_recv)
    me = y * 4 + x
    z_far = (8, 7, -7, 6, -6, 5, -5, 4, -4, 3, -3, 2, -2, 1, -1)

    def plane_sum(terms, arrived, mine, parts):
        total = terms[me].astype(jnp.float32)
        for slot in range(2 * CHIPS - 1):
            total += arrived[slot].astype(jnp.float32)
        mine[...] = total.astype(mine.dtype)
        wait_bytes(us.at[0:FSDP - 1], u_recv)

        for d in z_far:
            send(mine, parts.at[z], part_send, part_recv.at[half], along_z(d, home))

        @pl.when(at_home)
        def _():
            parts[z] = mine[...]

        @pl.when(jnp.logical_not(at_home))
        def _():
            send(mine, parts.at[z], part_send, part_recv.at[half], in_plane(0, 0, home))

    @pl.when(c == 0)
    def _():
        plane_sum(terms0, arrived0, mine0, parts0)

    @pl.when(c == 1)
    def _():
        plane_sum(terms1, arrived1, mine1, parts1)

    def sums(f):
        two = parts0[f].astype(jnp.float32) + parts0[f + FSDP].astype(jnp.float32)
        return two[0:ROWS], two[ROWS:2 * ROWS], parts1[f] + parts1[f + FSDP]

    def update(g, slot):
        low, high = sums(2 * g), sums(2 * g + 1)
        factor = outer_rate * (1.0 + outer_mu) / REPLICAS
        for j in range(3):
            cols = pl.ds(pl.multiple_of(first + j * LANES, LANES), LANES)
            pair = jnp.concatenate([us[2 * g, j] - factor * low[j], us[2 * g + 1, j] - factor * high[j]], axis=0)
            rows[slot, :, cols] = pair.astype(jnp.bfloat16)

    mine_cols = pl.ds(pl.multiple_of(first, LANES), SPAN)
    other_cols = slice(0, (CHIPS - 1) * SPAN)

    def spread(block, batch):
        for dx, dy in OFFSETS[:-1]:
            send(block, block, row_send.at[batch], row_recv.at[batch], in_plane(dx, dy, c))

    wait_bytes(arrived0.at[0:8], part_recv.at[1 - half])
    update(2 * (1 - half) + c, c)
    spread(rows.at[c, :, mine_cols], 0)

    @pl.when(at_home)
    def _():
        wait_bytes(arrived0.at[0:7], part_recv.at[half])
        update(2 * half + c, 3)
        for j, total in enumerate(sums(zl)):
            cols = pl.ds(pl.multiple_of(first + j * LANES, LANES), LANES)
            high = total.astype(jnp.bfloat16).astype(jnp.float32)
            rows[4, :, cols] = jnp.concatenate([high, total - high], axis=0).astype(jnp.bfloat16)
        spread(rows.at[3:5, :, mine_cols], 1)

    @pl.when(jnp.logical_not(at_home))
    def _():
        wait_bytes(arrived0.at[0:8], part_recv.at[half])
        update(2 * half + c, 2)
        spread(rows.at[2, :, mine_cols], 1)

    sibling = in_plane(0, 0, 1 - c)
    wait_bytes(rows.at[0, :, other_cols], row_recv.at[0])
    send(rows.at[c], rows.at[c], pass_send.at[0], pass_recv.at[0], sibling)

    @pl.when(at_home)
    def _():
        wait_bytes(rows.at[3:5, :, other_cols], row_recv.at[1])
        send(rows.at[3:5], rows.at[3:5], pass_send.at[1], pass_recv.at[1], sibling)
        wait_bytes(rows.at[2], pass_recv.at[1])

    @pl.when(jnp.logical_not(at_home))
    def _():
        wait_bytes(rows.at[2, :, other_cols], row_recv.at[1])
        send(rows.at[2], rows.at[2], pass_send.at[1], pass_recv.at[1], sibling)
        wait_bytes(rows.at[3:5], pass_recv.at[1])

    wait_bytes(rows.at[0], pass_recv.at[0])

    for j in range(COLS // LANES):
        cols = slice(j * LANES, (j + 1) * LANES)
        split = rows[4, :, cols].astype(jnp.float32)
        average = (split[0:ROWS] + split[ROWS:2 * ROWS]) / REPLICAS
        new_moment = outer_mu * moment[:, cols] + average
        new_moment_ref[:, cols] = new_moment
        new_base_ref[:, cols] = base[:, cols] - outer_rate * (average + outer_mu * new_moment)

    wait_bytes(arrived0, term_send)
    wait_bytes(us.at[0:FSDP - 1], u_send)
    wait_bytes(rows.at[0, :, other_cols], row_send.at[0])
    wait_bytes(rows.at[0], pass_send.at[0])

    @pl.when(at_home)
    def _():
        wait_bytes(arrived0.at[0:15], part_send)
        wait_bytes(rows.at[3:5, :, other_cols], row_send.at[1])
        wait_bytes(rows.at[3:5], pass_send.at[1])

    @pl.when(jnp.logical_not(at_home))
    def _():
        wait_bytes(arrived0.at[0:16], part_send)
        wait_bytes(rows.at[2, :, other_cols], row_send.at[1])
        wait_bytes(rows.at[2], pass_send.at[1])


def finish(new_base, new_moment, rows, new_base_out, new_moment_out, full_out, sems):
    zl = lax.axis_index("fsdp")
    half = zl // 4
    home = (zl // 2) % 2
    groups = (2 - 2 * half, 3 - 2 * half, 2 * half + 1 - home, 2 * half + home)
    copies = [(rows.at[slot], full_out.at[pl.ds(pl.multiple_of(16 * g, 16), 16)]) for slot, g in enumerate(groups)]
    copies += [(new_base, new_base_out), (new_moment, new_moment_out)]
    copies = [pltpu.make_async_copy(src, dst, sems.at[i]) for i, (src, dst) in enumerate(copies)]
    for copy in copies:
        copy.start()
    for copy in copies:
        copy.wait()


def step(local_weights, base_weights, momentum, scale_codes):
    anywhere = pl.BlockSpec(memory_space=pl.ANY)
    vmem = pl.BlockSpec(memory_space=pltpu.VMEM)
    dma = pltpu.SemaphoreType.DMA
    results = pl.pallas_call(
        kernel,
        out_shape=(
            pltpu.VMEM((ROWS, COLS), jnp.float32),
            pltpu.VMEM((ROWS, COLS), jnp.float32),
            pltpu.VMEM((5, 16, COLS), jnp.bfloat16),
        ),
        in_specs=[anywhere] * 4,
        out_specs=(vmem, vmem, vmem),
        scratch_shapes=[
            pltpu.VMEM((1, ROWS, COLS), jnp.bfloat16),
            pltpu.VMEM((ROWS, COLS), jnp.float32),
            pltpu.VMEM((ROWS, COLS), jnp.float32),
            pltpu.VMEM((1, ROWS, COLS // LANES), jnp.int32),
            pltpu.VMEM((CHIPS, 16, LANES), jnp.bfloat16),
            pltpu.VMEM((CHIPS, ROWS, LANES), jnp.float32),
            pltpu.VMEM((2 * CHIPS - 1, 16, LANES), jnp.bfloat16),
            pltpu.VMEM((2 * CHIPS - 1, ROWS, LANES), jnp.float32),
            pltpu.VMEM((16, LANES), jnp.bfloat16),
            pltpu.VMEM((ROWS, LANES), jnp.float32),
            pltpu.VMEM((Z, 16, LANES), jnp.bfloat16),
            pltpu.VMEM((Z, ROWS, LANES), jnp.float32),
            pltpu.VMEM((FSDP, 3, ROWS, LANES), jnp.float32),
            dma((4,)), dma, dma, dma, dma, dma, dma((2,)), dma((2,)), dma((2,)), dma((2,)), dma((2,)),
        ],
        compiler_params=pltpu.CompilerParams(collective_id=0, has_side_effects=True, vmem_limit_bytes=60 * 1024 * 1024),
        name="outer_step",
    )(*(pltpu.with_memory_space_constraint(a, pltpu.HBM) for a in (local_weights, base_weights, momentum, scale_codes)))
    return pl.pallas_call(
        finish,
        out_shape=(
            jax.ShapeDtypeStruct((ROWS, COLS), jnp.float32),
            jax.ShapeDtypeStruct((ROWS, COLS), jnp.float32),
            jax.ShapeDtypeStruct((FSDP * ROWS, COLS), jnp.bfloat16),
        ),
        in_specs=[anywhere] * 3,
        out_specs=(anywhere,) * 3,
        scratch_shapes=[dma((6,))],
        compiler_params=pltpu.CompilerParams(vmem_limit_bytes=1024 * 1024),
        name="write_out",
    )(*(pltpu.with_memory_space_constraint(r, pltpu.VMEM) for r in results))


def solution(mesh):
    in_specs = (P("rep", "fsdp", None), P("fsdp", None), P("fsdp", None), P("rep", "fsdp", None))
    out_specs = (P("fsdp", None), P("fsdp", None), P())
    return jax.shard_map(step, mesh=mesh, in_specs=in_specs, out_specs=out_specs, check_vma=False)
```

time: 47 us -> 38.9 us (0.83)
  Pallas kernels: 43.9 us -> 38.1 us
  local copies, waits for them, and re-layouts: 2.31 us -> 0 us
    pallas_call x1, Pallas kernels: 41.5 us -> 37 us  [step(): pl.pallas_call(kernel, out_shape=(pltpu.VMEM((ROWS, COLS), jnp.float32),...]
    unnamed x6 -> x0, local copies, waits for them, and re-layouts: 2.31 us -> none
    pallas_call x1, Pallas kernels: 2.43 us -> 1.07 us  [step(): pl.pallas_call(finish, out_shape=(jax.ShapeDtypeStruct((ROWS, COLS), jnp....]
where the time goes in v3:
time: 38.9 us; the launch traced here: 38.7 us
  Pallas kernels  38.1 us (98%)
  between operations  0.64 us (2%)
    pallas_call x1, Pallas kernels, step(): pl.pallas_call(kernel, out_shape=(pltpu.VMEM((ROWS, COLS), jnp.float32),...  37 us
    pallas_call x1, Pallas kernels, step(): pl.pallas_call(finish, out_shape=(jax.ShapeDtypeStruct((ROWS, COLS), jnp....  1.07 us

profile of v3, /device:TPU:1, one launch (start us, length us, event | category | flops | bytes accessed | tf_op | source)
XLA Modules:
  0.0 38.7 jit_solution(12464137272412655799)
XLA Ops:
  0.6 37.0 %outer_step.1 = (f32[8,6144]{1,0:T(8,128)S(1)}, f32[8,6144]{1,0:T(8,128)S(1)}, bf16[5,16,6144]{2,1,0:T(8,128)(2,1)S(1)}) custom-call(bf16[1,8,6144]{2,1,0:T(8,128)(2,1)} %local_hbm.1, f32[8,6144]{1,0:T(8,128)} %base_hbm.1, f32[8,6144]{1,0:T(8,128)} %moment_hbm.1, s32[1,8,48]{2,1,0:T(8,128)} %codes_hbm.1), custom_call_target="tpu_custom_call" | custom-call | tf_op jit(solution)/shard_map/outer_step/pallas_call | solution.py:246
  37.6 1.1 %write_out.1 = (f32[8,6144]{1,0:T(8,128)}, f32[8,6144]{1,0:T(8,128)}, bf16[64,6144]{1,0:T(8,128)(2,1)}) custom-call(f32[8,6144]{1,0:T(8,128)S(1)} %get-tuple-element.6.new_base, f32[8,6144]{1,0:T(8,128)S(1)} %get-tuple-element.7.new_moment, bf16[5,16,6144]{2,1,0:T(8,128)(2,1)S(1)} %get-tuple-element.8.rows), custom_call_target="tpu_custom_call" | custom-call | tf_op jit(solution)/shard_map/write_out/pallas_call | solution.py:274

commit v4 on v3

v4 whole, which is shorter than its diff:
```python
import jax
import jax.numpy as jnp
from jax import lax
from jax.experimental import pallas as pl
from jax.experimental.pallas import tpu as pltpu
from jax.sharding import PartitionSpec as P

outer_rate = 0.7
outer_mu = 0.9
clip_level = 4.0

ROWS = 8
COLS = 6144
LANES = 128
CHIPS = 16
SPAN = COLS // CHIPS
Z = 16
FSDP = 8
REPLICAS = 64
MESH = pl.DeviceIdType.MESH

OFFSETS = sorted(
    [(dx, dy) for dy in range(4) for dx in range(4)],
    key=lambda o: -(min(o[0], 4 - o[0]) + min(o[1], 4 - o[1])),
)


def wait_bytes(ref, sem):
    pltpu.make_async_copy(ref, ref, sem).wait()


def kernel(local_hbm, base_hbm, moment_hbm, codes_hbm, new_base_ref, new_moment_ref, rows,
           local, base, moment, codes, terms0, terms1, gotx0, gotx1, column0, column1, goty0, goty1, mine0, mine1,
           parts0, parts1, us, load_sem, greet_sem, x_send, x_recv, y_send, y_recv, u_send, u_recv, part_send, part_recv, row_send, row_recv, pass_send, pass_recv):
    rep = lax.axis_index("rep")
    zl = lax.axis_index("fsdp")
    c = rep % 2
    x = (rep // 2) % 4
    zh = (rep // 8) % 2
    y = rep // 16
    z = zh * FSDP + zl
    half = zl // 4
    home = (zl // 2) % 2
    at_home = c == home
    first = (y * 4 + x) * SPAN
    xs = [(x + d) % 4 for d in range(4)]
    ys = [(y + d) % 4 for d in range(4)]

    def in_plane(dx, dy, pc):
        return (ys[dy] * 16 + zh * 8 + xs[dx] * 2 + pc, zl)

    def along_z(d, pc):
        zt = (z + d + Z) % Z
        return (y * 16 + (zt // FSDP) * 8 + x * 2 + pc, zt % FSDP)

    def send(src, dst, send_sem, recv_sem, to):
        pltpu.make_async_remote_copy(
            src_ref=src, dst_ref=dst, send_sem=send_sem, recv_sem=recv_sem, device_id=to, device_id_type=MESH).start()

    loads = [
        pltpu.make_async_copy(src, dst, load_sem.at[i])
        for i, (src, dst) in enumerate(((codes_hbm, codes), (local_hbm, local), (base_hbm, base), (moment_hbm, moment)))
    ]
    for load in loads:
        load.start()

    barrier = pltpu.get_barrier_semaphore()
    greeted = [along_z(d, pc) for d in (2, -2) for pc in (c, 1 - c)]
    greeted += [in_plane(2, 0, c), in_plane(2, 0, 1 - c), in_plane(0, 2, c)]
    greeted += [along_z(d, pc) for d in (1, -1) for pc in (c, 1 - c)]
    greeted += [in_plane(dx, 0, pc) for dx in (1, 3) for pc in (c, 1 - c)]
    greeted += [in_plane(0, 1, c), in_plane(0, 3, c), in_plane(0, 0, 1 - c)]
    for peer in greeted:
        pl.semaphore_signal(barrier, inc=1, device_id=peer, device_id_type=MESH)

    for load in loads:
        load.wait()

    scales = codes[0].astype(jnp.float32) / 64.0
    inverse = 1.0 / scales

    def term(j):
        cols = slice(j * LANES, (j + 1) * LANES)
        pseudo = base[:, cols] - local[0, :, cols].astype(jnp.float32)
        quantized = jnp.clip(pseudo * inverse[:, j:j + 1], -clip_level, clip_level).astype(jnp.bfloat16)
        return quantized.astype(jnp.float32) * scales[:, j:j + 1]

    for k in range(CHIPS):
        to_y, to_x = k // 4, k % 4
        terms0[to_x, to_y] = jnp.concatenate([term(3 * k), term(3 * k + 1)], axis=0).astype(jnp.bfloat16)
        terms1[to_x, to_y] = term(3 * k + 2)

    for j in range(3):
        cols = pl.ds(pl.multiple_of(first + j * LANES, LANES), LANES)
        us[zl, j] = base[:, cols] - (outer_rate * outer_mu * outer_mu) * moment[:, cols]

    pl.semaphore_wait(barrier, len(greeted))

    for d in (2, -2):
        pl.semaphore_signal(greet_sem.at[0], inc=1, device_id=along_z(d, c), device_id_type=MESH)
    for dx in (2, 1, 3):
        send(terms0.at[xs[dx]], gotx0.at[2 * dx - 1 + c], x_send, x_recv, in_plane(dx, 0, 0))
        send(terms1.at[xs[dx]], gotx1.at[2 * dx - c], x_send, x_recv, in_plane(dx, 0, 1))

    @pl.when(c == 1)
    def _():
        send(terms0.at[x], gotx0.at[0], x_send, x_recv, in_plane(0, 0, 0))

    @pl.when(c == 0)
    def _():
        send(terms1.at[x], gotx1.at[0], x_send, x_recv, in_plane(0, 0, 1))

    pl.semaphore_wait(greet_sem.at[0], 2)
    for d in (4, -4):
        pl.semaphore_signal(greet_sem.at[1], inc=1, device_id=along_z(d, c), device_id_type=MESH)
    for d in (4, 3, -3, 2, -2, 1, -1):
        send(us.at[zl], us.at[zl], u_send, u_recv, along_z(d, c))

    wait_bytes(gotx0, x_recv)
    z_far = (7, -7, 6, -6, 5, -5, 4, -4, 3, -3, 2, -2, 1, -1)

    def plane_sum(terms, gotx, column, goty, mine, parts):
        for dy in (2, 1, 3, 0):
            total = terms[x, ys[dy]].astype(jnp.float32)
            for slot in range(7):
                total += gotx[slot, ys[dy]].astype(jnp.float32)
            if dy:
                column[dy - 1] = total.astype(column.dtype)
                send(column.at[dy - 1], goty.at[dy - 1], y_send, y_recv, in_plane(0, dy, c))
        wait_bytes(goty, y_recv)
        for slot in range(3):
            total += goty[slot].astype(jnp.float32)
        mine[...] = total.astype(mine.dtype)
        pl.semaphore_wait(greet_sem.at[1], 2)

        send(mine, parts.at[z], part_send, part_recv.at[2], along_z(8, 1 - home))
        for i in range(Z - 1):
            zt = i + jnp.where(i >= z, 1, 0)
            to = (y * 16 + (zt // FSDP) * 8 + x * 2 + home, zt % FSDP)
            send(mine, parts.at[z], part_send, part_recv.at[half], to)
        send(mine, parts.at[z], part_send, part_recv.at[jnp.where(at_home, 2, half)], in_plane(0, 0, 1 - c))
        parts[z] = mine[...]

    @pl.when(c == 0)
    def _():
        plane_sum(terms0, gotx0, column0, goty0, mine0, parts0)

    @pl.when(c == 1)
    def _():
        plane_sum(terms1, gotx1, column1, goty1, mine1, parts1)

    def sums(f):
        two = parts0[f].astype(jnp.float32) + parts0[f + FSDP].astype(jnp.float32)
        return two[0:ROWS], two[ROWS:2 * ROWS], parts1[f] + parts1[f + FSDP]

    me = y * 4 + x

    def my_lanes(j):
        return pl.ds(pl.multiple_of(first + j * LANES, LANES), LANES)

    def group(g):
        return pl.ds(pl.multiple_of(16 * g, 16), 16)

    def update(g):
        low, high = sums(2 * g), sums(2 * g + 1)
        factor = outer_rate * (1.0 + outer_mu) / REPLICAS
        for j in range(3):
            pair = jnp.concatenate([us[2 * g, j] - factor * low[j], us[2 * g + 1, j] - factor * high[j]], axis=0)
            rows[group(g), my_lanes(j)] = pair.astype(jnp.bfloat16)

    mine_cols = pl.ds(pl.multiple_of(first, LANES), SPAN)
    other_cols = slice(0, (CHIPS - 1) * SPAN)
    split_rows = slice(64, 80)

    def spread(part, batch):
        block = rows.at[part, mine_cols]
        for i in range(CHIPS - 1):
            k = i + jnp.where(i >= me, 1, 0)
            to = ((k // 4) * 16 + zh * 8 + (k % 4) * 2 + c, zl)
            send(block, block, row_send.at[batch], row_recv.at[batch], to)

    wait_bytes(us.at[0:FSDP - 1], u_recv)
    near, far = 2 * (1 - half) + c, 2 * half + c
    wait_bytes(parts0.at[0:8], part_recv.at[1 - half])
    update(near)
    spread(group(near), 0)

    @pl.when(at_home)
    def _():
        wait_bytes(parts0.at[0:7], part_recv.at[half])
        update(far)
        spread(group(far), 1)

    @pl.when(jnp.logical_not(at_home))
    def _():
        wait_bytes(parts0.at[0:8], part_recv.at[half])
        update(far)
        spread(group(far), 1)
        wait_bytes(parts0.at[0:3], part_recv.at[2])
        for j, total in enumerate(sums(zl)):
            high = total.astype(jnp.bfloat16).astype(jnp.float32)
            rows[split_rows, my_lanes(j)] = jnp.concatenate([high, total - high], axis=0).astype(jnp.bfloat16)
        spread(split_rows, 2)

    any_rows = rows.at[0:16]
    other_rows = rows.at[0:16, other_cols]

    def pass_on(part, batch):
        wait_bytes(other_rows, row_recv.at[batch])
        send(rows.at[part], rows.at[part], pass_send.at[batch], pass_recv.at[batch], in_plane(0, 0, 1 - c))

    pass_on(group(near), 0)
    pass_on(group(far), 1)

    @pl.when(at_home)
    def _():
        wait_bytes(any_rows, pass_recv.at[2])

    @pl.when(jnp.logical_not(at_home))
    def _():
        pass_on(split_rows, 2)

    for j in range(COLS // LANES):
        cols = slice(j * LANES, (j + 1) * LANES)
        split = rows[split_rows, cols].astype(jnp.float32)
        average = (split[0:ROWS] + split[ROWS:2 * ROWS]) / REPLICAS
        new_moment = outer_mu * moment[:, cols] + average
        new_moment_ref[:, cols] = new_moment
        new_base_ref[:, cols] = base[:, cols] - outer_rate * (average + outer_mu * new_moment)

    for batch in range(2):
        wait_bytes(any_rows, pass_recv.at[batch])
    wait_bytes(gotx0, x_send)
    wait_bytes(goty0, y_send)
    wait_bytes(us.at[0:FSDP - 1], u_send)
    wait_bytes(parts0, part_send)
    wait_bytes(parts0.at[0:1], part_send)
    for batch in range(2):
        wait_bytes(other_rows, row_send.at[batch])
        wait_bytes(any_rows, pass_send.at[batch])

    @pl.when(jnp.logical_not(at_home))
    def _():
        wait_bytes(other_rows, row_send.at[2])
        wait_bytes(any_rows, pass_send.at[2])


def finish(new_base, new_moment, rows, new_base_out, new_moment_out, full_out, sems):
    copies = [(rows.at[0:64], full_out), (new_base, new_base_out), (new_moment, new_moment_out)]
    copies = [pltpu.make_async_copy(src, dst, sems.at[i]) for i, (src, dst) in enumerate(copies)]
    for copy in copies:
        copy.start()
    for copy in copies:
        copy.wait()


def step(local_weights, base_weights, momentum, scale_codes):
    anywhere = pl.BlockSpec(memory_space=pl.ANY)
    vmem = pl.BlockSpec(memory_space=pltpu.VMEM)
    dma = pltpu.SemaphoreType.DMA
    results = pl.pallas_call(
        kernel,
        out_shape=(
            pltpu.VMEM((ROWS, COLS), jnp.float32),
            pltpu.VMEM((ROWS, COLS), jnp.float32),
            pltpu.VMEM((80, COLS), jnp.bfloat16),
        ),
        in_specs=[anywhere] * 4,
        out_specs=(vmem, vmem, vmem),
        scratch_shapes=[
            pltpu.VMEM((1, ROWS, COLS), jnp.bfloat16),
            pltpu.VMEM((ROWS, COLS), jnp.float32),
            pltpu.VMEM((ROWS, COLS), jnp.float32),
            pltpu.VMEM((1, ROWS, COLS // LANES), jnp.int32),
            pltpu.VMEM((4, 4, 16, LANES), jnp.bfloat16),
            pltpu.VMEM((4, 4, ROWS, LANES), jnp.float32),
            pltpu.VMEM((7, 4, 16, LANES), jnp.bfloat16),
            pltpu.VMEM((7, 4, ROWS, LANES), jnp.float32),
            pltpu.VMEM((3, 16, LANES), jnp.bfloat16),
            pltpu.VMEM((3, ROWS, LANES), jnp.float32),
            pltpu.VMEM((3, 16, LANES), jnp.bfloat16),
            pltpu.VMEM((3, ROWS, LANES), jnp.float32),
            pltpu.VMEM((16, LANES), jnp.bfloat16),
            pltpu.VMEM((ROWS, LANES), jnp.float32),
            pltpu.VMEM((Z, 16, LANES), jnp.bfloat16),
            pltpu.VMEM((Z, ROWS, LANES), jnp.float32),
            pltpu.VMEM((FSDP, 3, ROWS, LANES), jnp.float32),
            dma((4,)), pltpu.SemaphoreType.REGULAR((2,)), dma, dma, dma, dma, dma, dma, dma, dma((3,)), dma((3,)), dma((3,)), dma((3,)), dma((3,)),
        ],
        compiler_params=pltpu.CompilerParams(collective_id=0, has_side_effects=True, vmem_limit_bytes=60 * 1024 * 1024),
        name="outer_step",
    )(*(pltpu.with_memory_space_constraint(a, pltpu.HBM) for a in (local_weights, base_weights, momentum, scale_codes)))
    return pl.pallas_call(
        finish,
        out_shape=(
            jax.ShapeDtypeStruct((ROWS, COLS), jnp.float32),
            jax.ShapeDtypeStruct((ROWS, COLS), jnp.float32),
            jax.ShapeDtypeStruct((FSDP * ROWS, COLS), jnp.bfloat16),
        ),
        in_specs=[anywhere] * 3,
        out_specs=(anywhere,) * 3,
        scratch_shapes=[dma((3,))],
        compiler_params=pltpu.CompilerParams(vmem_limit_bytes=1024 * 1024),
        name="write_out",
    )(*(pltpu.with_memory_space_constraint(r, pltpu.VMEM) for r in results))


def solution(mesh):
    in_specs = (P("rep", "fsdp", None), P("fsdp", None), P("fsdp", None), P("rep", "fsdp", None))
    out_specs = (P("fsdp", None), P("fsdp", None), P())
    return jax.shard_map(step, mesh=mesh, in_specs=in_specs, out_specs=out_specs, check_vma=False)
```

time: 38.9 us -> 37.9 us (0.974)
  Pallas kernels: 38.1 us -> 37.1 us
    pallas_call x1, Pallas kernels: 37 us -> 36.1 us  [step(): pl.pallas_call(kernel, out_shape=(pltpu.VMEM((ROWS, COLS), jnp.float32),...]
where the time goes in v4:
time: 37.9 us; the launch traced here: 37.7 us
  Pallas kernels  37.1 us (98%)
  between operations  0.64 us (2%)
    pallas_call x1, Pallas kernels, step(): pl.pallas_call(kernel, out_shape=(pltpu.VMEM((ROWS, COLS), jnp.float32),...  36.1 us
    pallas_call x1, Pallas kernels, step(): pl.pallas_call(finish, out_shape=(jax.ShapeDtypeStruct((ROWS, COLS), jnp....  1.03 us

profile of v4, /device:TPU:1, one launch (start us, length us, event | category | flops | bytes accessed | tf_op | source)
XLA Modules:
  0.0 37.7 jit_solution(6070042049543584132)
XLA Ops:
  0.6 36.1 %outer_step.1 = (f32[8,6144]{1,0:T(8,128)S(1)}, f32[8,6144]{1,0:T(8,128)S(1)}, bf16[80,6144]{1,0:T(8,128)(2,1)S(1)}) custom-call(bf16[1,8,6144]{2,1,0:T(8,128)(2,1)} %local_hbm.1, f32[8,6144]{1,0:T(8,128)} %base_hbm.1, f32[8,6144]{1,0:T(8,128)} %moment_hbm.1, s32[1,8,48]{2,1,0:T(8,128)} %codes_hbm.1), custom_call_target="tpu_custom_call" | custom-call | tf_op jit(solution)/shard_map/outer_step/pallas_call | solution.py:261
  36.7 1.0 %write_out.1 = (f32[8,6144]{1,0:T(8,128)}, f32[8,6144]{1,0:T(8,128)}, bf16[64,6144]{1,0:T(8,128)(2,1)}) custom-call(f32[8,6144]{1,0:T(8,128)S(1)} %get-tuple-element.6.new_base, f32[8,6144]{1,0:T(8,128)S(1)} %get-tuple-element.7.new_moment, bf16[80,6144]{1,0:T(8,128)(2,1)S(1)} %get-tuple-element.8.rows), custom_call_target="tpu_custom_call" | custom-call | tf_op jit(solution)/shard_map/write_out/pallas_call | solution.py:293

commit v5 on v4

--- a/solution.py
+++ b/solution.py
@@ -30,8 +30,8 @@
 
 
 def kernel(local_hbm, base_hbm, moment_hbm, codes_hbm, new_base_ref, new_moment_ref, rows,
-           local, base, moment, codes, terms0, terms1, gotx0, gotx1, column0, column1, goty0, goty1, mine0, mine1,
-           parts0, parts1, us, load_sem, greet_sem, x_send, x_recv, y_send, y_recv, u_send, u_recv, part_send, part_recv, row_send, row_recv, pass_send, pass_recv):
+           local, base, moment, codes, terms0, terms1, arrived0, arrived1, mine0, mine1,
+           parts0, parts1, us, load_sem, greet_sem, x_send, x_recv, u_send, u_recv, part_send, part_recv, row_send, row_recv, pass_send, pass_recv):
     rep = lax.axis_index("rep")
     zl = lax.axis_index("fsdp")
     c = rep % 2
@@ -65,11 +65,12 @@
         load.start()
 
     barrier = pltpu.get_barrier_semaphore()
-    greeted = [along_z(d, pc) for d in (2, -2) for pc in (c, 1 - c)]
-    greeted += [in_plane(2, 0, c), in_plane(2, 0, 1 - c), in_plane(0, 2, c)]
+    greeted = [in_plane(dx, dy, pc) for dx, dy in OFFSETS[:5] for pc in (c, 1 - c)]
+    greeted += [along_z(d, pc) for d in (2, -2) for pc in (c, 1 - c)]
+    greeted += [in_plane(dx, dy, pc) for dx, dy in OFFSETS[5:11] for pc in (c, 1 - c)]
     greeted += [along_z(d, pc) for d in (1, -1) for pc in (c, 1 - c)]
-    greeted += [in_plane(dx, 0, pc) for dx in (1, 3) for pc in (c, 1 - c)]
-    greeted += [in_plane(0, 1, c), in_plane(0, 3, c), in_plane(0, 0, 1 - c)]
+    greeted += [in_plane(dx, dy, pc) for dx, dy in OFFSETS[11:15] for pc in (c, 1 - c)]
+    greeted += [in_plane(0, 0, 1 - c)]
     for peer in greeted:
         pl.semaphore_signal(barrier, inc=1, device_id=peer, device_id_type=MESH)
 
@@ -86,9 +87,8 @@
         return quantized.astype(jnp.float32) * scales[:, j:j + 1]
 
     for k in range(CHIPS):
-        to_y, to_x = k // 4, k % 4
-        terms0[to_x, to_y] = jnp.concatenate([term(3 * k), term(3 * k + 1)], axis=0).astype(jnp.bfloat16)
-        terms1[to_x, to_y] = term(3 * k + 2)
+        terms0[k] = jnp.concatenate([term(3 * k), term(3 * k + 1)], axis=0).astype(jnp.bfloat16)
+        terms1[k] = term(3 * k + 2)
 
     for j in range(3):
         cols = pl.ds(pl.multiple_of(first + j * LANES, LANES), LANES)
@@ -98,17 +98,22 @@
 
     for d in (2, -2):
         pl.semaphore_signal(greet_sem.at[0], inc=1, device_id=along_z(d, c), device_id_type=MESH)
-    for dx in (2, 1, 3):
-        send(terms0.at[xs[dx]], gotx0.at[2 * dx - 1 + c], x_send, x_recv, in_plane(dx, 0, 0))
-        send(terms1.at[xs[dx]], gotx1.at[2 * dx - c], x_send, x_recv, in_plane(dx, 0, 1))
+
+    for dx, dy in OFFSETS[:-1]:
+        k = ys[dy] * 4 + xs[dx]
+        slot = (dy * 4 + dx) * 2 - 1
+        send(terms0.at[k], arrived0.at[slot + c], x_send, x_recv, in_plane(dx, dy, 0))
+        send(terms1.at[k], arrived1.at[slot + 1 - c], x_send, x_recv, in_plane(dx, dy, 1))
+
+    me = y * 4 + x
 
     @pl.when(c == 1)
     def _():
-        send(terms0.at[x], gotx0.at[0], x_send, x_recv, in_plane(0, 0, 0))
+        send(terms0.at[me], arrived0.at[0], x_send, x_recv, in_plane(0, 0, 0))
 
     @pl.when(c == 0)
     def _():
-        send(terms1.at[x], gotx1.at[0], x_send, x_recv, in_plane(0, 0, 1))
+        send(terms1.at[me], arrived1.at[0], x_send, x_recv, in_plane(0, 0, 1))
 
     pl.semaphore_wait(greet_sem.at[0], 2)
     for d in (4, -4):
@@ -116,20 +121,13 @@
     for d in (4, 3, -3, 2, -2, 1, -1):
         send(us.at[zl], us.at[zl], u_send, u_recv, along_z(d, c))
 
-    wait_bytes(gotx0, x_recv)
+    wait_bytes(arrived0, x_recv)
     z_far = (7, -7, 6, -6, 5, -5, 4, -4, 3, -3, 2, -2, 1, -1)
 
-    def plane_sum(terms, gotx, column, goty, mine, parts):
-        for dy in (2, 1, 3, 0):
-            total = terms[x, ys[dy]].astype(jnp.float32)
-            for slot in range(7):
-                total += gotx[slot, ys[dy]].astype(jnp.float32)
-            if dy:
-                column[dy - 1] = total.astype(column.dtype)
-                send(column.at[dy - 1], goty.at[dy - 1], y_send, y_recv, in_plane(0, dy, c))
-        wait_bytes(goty, y_recv)
-        for slot in range(3):
-            total += goty[slot].astype(jnp.float32)
+    def plane_sum(terms, arrived, mine, parts):
+        total = terms[me].astype(jnp.float32)
+        for slot in range(2 * CHIPS - 1):
+            total += arrived[slot].astype(jnp.float32)
         mine[...] = total.astype(mine.dtype)
         pl.semaphore_wait(greet_sem.at[1], 2)
 
@@ -143,17 +141,15 @@
 
     @pl.when(c == 0)
     def _():
-        plane_sum(terms0, gotx0, column0, goty0, mine0, parts0)
+        plane_sum(terms0, arrived0, mine0, parts0)
 
     @pl.when(c == 1)
     def _():
-        plane_sum(terms1, gotx1, column1, goty1, mine1, parts1)
+        plane_sum(terms1, arrived1, mine1, parts1)
 
     def sums(f):
         two = parts0[f].astype(jnp.float32) + parts0[f + FSDP].astype(jnp.float32)
         return two[0:ROWS], two[ROWS:2 * ROWS], parts1[f] + parts1[f + FSDP]
-
-    me = y * 4 + x
 
     def my_lanes(j):
         return pl.ds(pl.multiple_of(first + j * LANES, LANES), LANES)
@@ -230,8 +226,7 @@
 
     for batch in range(2):
         wait_bytes(any_rows, pass_recv.at[batch])
-    wait_bytes(gotx0, x_send)
-    wait_bytes(goty0, y_send)
+    wait_bytes(arrived0, x_send)
     wait_bytes(us.at[0:FSDP - 1], u_send)
     wait_bytes(parts0, part_send)
     wait_bytes(parts0.at[0:1], part_send)
@@ -272,20 +267,16 @@
             pltpu.VMEM((ROWS, COLS), jnp.float32),
             pltpu.VMEM((ROWS, COLS), jnp.float32),
             pltpu.VMEM((1, ROWS, COLS // LANES), jnp.int32),
-            pltpu.VMEM((4, 4, 16, LANES), jnp.bfloat16),
-            pltpu.VMEM((4, 4, ROWS, LANES), jnp.float32),
-            pltpu.VMEM((7, 4, 16, LANES), jnp.bfloat16),
-            pltpu.VMEM((7, 4, ROWS, LANES), jnp.float32),
-            pltpu.VMEM((3, 16, LANES), jnp.bfloat16),
-            pltpu.VMEM((3, ROWS, LANES), jnp.float32),
-            pltpu.VMEM((3, 16, LANES), jnp.bfloat16),
-            pltpu.VMEM((3, ROWS, LANES), jnp.float32),
+            pltpu.VMEM((CHIPS, 16, LANES), jnp.bfloat16),
+            pltpu.VMEM((CHIPS, ROWS, LANES), jnp.float32),
+            pltpu.VMEM((2 * CHIPS - 1, 16, LANES), jnp.bfloat16),
+            pltpu.VMEM((2 * CHIPS - 1, ROWS, LANES), jnp.float32),
             pltpu.VMEM((16, LANES), jnp.bfloat16),
             pltpu.VMEM((ROWS, LANES), jnp.float32),
             pltpu.VMEM((Z, 16, LANES), jnp.bfloat16),
             pltpu.VMEM((Z, ROWS, LANES), jnp.float32),
             pltpu.VMEM((FSDP, 3, ROWS, LANES), jnp.float32),
-            dma((4,)), pltpu.SemaphoreType.REGULAR((2,)), dma, dma, dma, dma, dma, dma, dma, dma((3,)), dma((3,)), dma((3,)), dma((3,)), dma((3,)),
+            dma((4,)), pltpu.SemaphoreType.REGULAR((2,)), dma, dma, dma, dma, dma, dma((3,)), dma((3,)), dma((3,)), dma((3,)), dma((3,)),
         ],
         compiler_params=pltpu.CompilerParams(collective_id=0, has_side_effects=True, vmem_limit_bytes=60 * 1024 * 1024),
         name="outer_step",

time: 37.9 us -> 36.8 us (0.971)
  Pallas kernels: 37.1 us -> 36 us
    pallas_call x1, Pallas kernels: 36.1 us -> 35 us  [step(): pl.pallas_call(kernel, out_shape=(pltpu.VMEM((ROWS, COLS), jnp.float32),...]
where the time goes in v5:
time: 36.8 us; the launch traced here: 36.6 us
  Pallas kernels  36 us (98%)
  between operations  0.64 us (2%)
    pallas_call x1, Pallas kernels, step(): pl.pallas_call(kernel, out_shape=(pltpu.VMEM((ROWS, COLS), jnp.float32),...  35 us
    pallas_call x1, Pallas kernels, step(): pl.pallas_call(finish, out_shape=(jax.ShapeDtypeStruct((ROWS, COLS), jnp....  1.03 us

profile of v5, /device:TPU:1, one launch (start us, length us, event | category | flops | bytes accessed | tf_op | source)
XLA Modules:
  0.0 36.6 jit_solution(5329075958640880028)
XLA Ops:
  0.6 35.0 %outer_step.1 = (f32[8,6144]{1,0:T(8,128)S(1)}, f32[8,6144]{1,0:T(8,128)S(1)}, bf16[80,6144]{1,0:T(8,128)(2,1)S(1)}) custom-call(bf16[1,8,6144]{2,1,0:T(8,128)(2,1)} %local_hbm.1, f32[8,6144]{1,0:T(8,128)} %base_hbm.1, f32[8,6144]{1,0:T(8,128)} %moment_hbm.1, s32[1,8,48]{2,1,0:T(8,128)} %codes_hbm.1), custom_call_target="tpu_custom_call" | custom-call | tf_op jit(solution)/shard_map/outer_step/pallas_call | solution.py:256
  35.6 1.0 %write_out.1 = (f32[8,6144]{1,0:T(8,128)}, f32[8,6144]{1,0:T(8,128)}, bf16[64,6144]{1,0:T(8,128)(2,1)}) custom-call(f32[8,6144]{1,0:T(8,128)S(1)} %get-tuple-element.6.new_base, f32[8,6144]{1,0:T(8,128)S(1)} %get-tuple-element.7.new_moment, bf16[80,6144]{1,0:T(8,128)(2,1)S(1)} %get-tuple-element.8.rows), custom_call_target="tpu_custom_call" | custom-call | tf_op jit(solution)/shard_map/write_out/pallas_call | solution.py:284

commit v6 on v5

--- a/solution.py
+++ b/solution.py
@@ -18,6 +18,7 @@
 FSDP = 8
 REPLICAS = 64
 MESH = pl.DeviceIdType.MESH
+FIRST = 11
 
 OFFSETS = sorted(
     [(dx, dy) for dy in range(4) for dx in range(4)],
@@ -65,12 +66,10 @@
         load.start()
 
     barrier = pltpu.get_barrier_semaphore()
-    greeted = [in_plane(dx, dy, pc) for dx, dy in OFFSETS[:5] for pc in (c, 1 - c)]
-    greeted += [along_z(d, pc) for d in (2, -2) for pc in (c, 1 - c)]
-    greeted += [in_plane(dx, dy, pc) for dx, dy in OFFSETS[5:11] for pc in (c, 1 - c)]
-    greeted += [along_z(d, pc) for d in (1, -1) for pc in (c, 1 - c)]
-    greeted += [in_plane(dx, dy, pc) for dx, dy in OFFSETS[11:15] for pc in (c, 1 - c)]
-    greeted += [in_plane(0, 0, 1 - c)]
+    greeted = [in_plane(dx, dy, c) for dx, dy in OFFSETS[:5]]
+    greeted += [along_z(2, c), along_z(-2, c)]
+    greeted += [in_plane(dx, dy, c) for dx, dy in OFFSETS[5:15]]
+    greeted += [along_z(1, c), along_z(-1, c), in_plane(0, 0, 1 - c)]
     for peer in greeted:
         pl.semaphore_signal(barrier, inc=1, device_id=peer, device_id_type=MESH)
 
@@ -96,14 +95,28 @@
 
     pl.semaphore_wait(barrier, len(greeted))
 
+    pl.semaphore_signal(greet_sem.at[2], inc=1, device_id=in_plane(0, 0, 1 - c), device_id_type=MESH)
+
+    def to_core(offsets, pc):
+        @pl.when(pc == 0)
+        def _():
+            for dx, dy in offsets:
+                slot = (dy * 4 + dx) * 2 - 1
+                send(terms0.at[ys[dy] * 4 + xs[dx]], arrived0.at[slot + c], x_send, x_recv, in_plane(dx, dy, 0))
+
+        @pl.when(pc == 1)
+        def _():
+            for dx, dy in offsets:
+                slot = (dy * 4 + dx) * 2 - 1
+                send(terms1.at[ys[dy] * 4 + xs[dx]], arrived1.at[slot + 1 - c], x_send, x_recv, in_plane(dx, dy, 1))
+
+    to_core(OFFSETS[:FIRST], c)
+    pl.semaphore_wait(greet_sem.at[2], 1)
     for d in (2, -2):
         pl.semaphore_signal(greet_sem.at[0], inc=1, device_id=along_z(d, c), device_id_type=MESH)
-
-    for dx, dy in OFFSETS[:-1]:
-        k = ys[dy] * 4 + xs[dx]
-        slot = (dy * 4 + dx) * 2 - 1
-        send(terms0.at[k], arrived0.at[slot + c], x_send, x_recv, in_plane(dx, dy, 0))
-        send(terms1.at[k], arrived1.at[slot + 1 - c], x_send, x_recv, in_plane(dx, dy, 1))
+    to_core(OFFSETS[:FIRST], 1 - c)
+    to_core(OFFSETS[FIRST:-1], c)
+    to_core(OFFSETS[FIRST:-1], 1 - c)
 
     me = y * 4 + x
 
@@ -276,7 +289,7 @@
             pltpu.VMEM((Z, 16, LANES), jnp.bfloat16),
             pltpu.VMEM((Z, ROWS, LANES), jnp.float32),
             pltpu.VMEM((FSDP, 3, ROWS, LANES), jnp.float32),
-            dma((4,)), pltpu.SemaphoreType.REGULAR((2,)), dma, dma, dma, dma, dma, dma((3,)), dma((3,)), dma((3,)), dma((3,)), dma((3,)),
+            dma((4,)), pltpu.SemaphoreType.REGULAR((3,)), dma, dma, dma, dma, dma, dma((3,)), dma((3,)), dma((3,)), dma((3,)), dma((3,)),
         ],
         compiler_params=pltpu.CompilerParams(collective_id=0, has_side_effects=True, vmem_limit_bytes=60 * 1024 * 1024),
         name="outer_step",

time: 36.8 us -> 36.8 us (level)
  no operation moved by 1% of the time
where the time goes in v6:
time: 36.8 us; the launch traced here: 36.6 us
  Pallas kernels  36 us (98%)
  between operations  0.64 us (2%)
    pallas_call x1, Pallas kernels, step(): pl.pallas_call(kernel, out_shape=(pltpu.VMEM((ROWS, COLS), jnp.float32),...  35 us
    pallas_call x1, Pallas kernels, step(): pl.pallas_call(finish, out_shape=(jax.ShapeDtypeStruct((ROWS, COLS), jnp....  1.03 us

profile of v6, /device:TPU:1, one launch (start us, length us, event | category | flops | bytes accessed | tf_op | source)
XLA Modules:
  0.0 36.6 jit_solution(7695830221390009934)
XLA Ops:
  0.6 35.0 %outer_step.1 = (f32[8,6144]{1,0:T(8,128)S(1)}, f32[8,6144]{1,0:T(8,128)S(1)}, bf16[80,6144]{1,0:T(8,128)(2,1)S(1)}) custom-call(bf16[1,8,6144]{2,1,0:T(8,128)(2,1)} %local_hbm.1, f32[8,6144]{1,0:T(8,128)} %base_hbm.1, f32[8,6144]{1,0:T(8,128)} %moment_hbm.1, s32[1,8,48]{2,1,0:T(8,128)} %codes_hbm.1), custom_call_target="tpu_custom_call" | custom-call | tf_op jit(solution)/shard_map/outer_step/pallas_call | solution.py:269
  35.6 1.0 %write_out.1 = (f32[8,6144]{1,0:T(8,128)}, f32[8,6144]{1,0:T(8,128)}, bf16[64,6144]{1,0:T(8,128)(2,1)}) custom-call(f32[8,6144]{1,0:T(8,128)S(1)} %get-tuple-element.6.new_base, f32[8,6144]{1,0:T(8,128)S(1)} %get-tuple-element.7.new_moment, bf16[80,6144]{1,0:T(8,128)(2,1)S(1)} %get-tuple-element.8.rows), custom_call_target="tpu_custom_call" | custom-call | tf_op jit(solution)/shard_map/write_out/pallas_call | solution.py:297

commit v7 on v6

--- a/solution.py
+++ b/solution.py
@@ -62,16 +62,16 @@
         pltpu.make_async_copy(src, dst, load_sem.at[i])
         for i, (src, dst) in enumerate(((codes_hbm, codes), (local_hbm, local), (base_hbm, base), (moment_hbm, moment)))
     ]
-    for load in loads:
-        load.start()
-
     barrier = pltpu.get_barrier_semaphore()
     greeted = [in_plane(dx, dy, c) for dx, dy in OFFSETS[:5]]
     greeted += [along_z(2, c), along_z(-2, c)]
     greeted += [in_plane(dx, dy, c) for dx, dy in OFFSETS[5:15]]
     greeted += [along_z(1, c), along_z(-1, c), in_plane(0, 0, 1 - c)]
-    for peer in greeted:
+    for i, peer in enumerate(greeted):
         pl.semaphore_signal(barrier, inc=1, device_id=peer, device_id_type=MESH)
+        if i == 6:
+            for load in loads:
+                load.start()
 
     for load in loads:
         load.wait()
@@ -186,7 +186,7 @@
         for i in range(CHIPS - 1):
             k = i + jnp.where(i >= me, 1, 0)
             to = ((k // 4) * 16 + zh * 8 + (k % 4) * 2 + c, zl)
-            send(block, block, row_send.at[batch], row_recv.at[batch], to)
+            send(block, block, row_send.at[batch], row_recv.at[2 * batch + me // 8], to)
 
     wait_bytes(us.at[0:FSDP - 1], u_recv)
     near, far = 2 * (1 - half) + c, 2 * half + c
@@ -215,8 +215,19 @@
     other_rows = rows.at[0:16, other_cols]
 
     def pass_on(part, batch):
-        wait_bytes(other_rows, row_recv.at[batch])
-        send(rows.at[part], rows.at[part], pass_send.at[batch], pass_recv.at[batch], in_plane(0, 0, 1 - c))
+        for upper in range(2):
+            arrival = row_recv.at[2 * batch + upper]
+
+            @pl.when(me // 8 == upper)
+            def _():
+                wait_bytes(rows.at[0:16, 0:7 * SPAN], arrival)
+
+            @pl.when(me // 8 != upper)
+            def _():
+                wait_bytes(rows.at[0:16, 0:8 * SPAN], arrival)
+
+            block = rows.at[part, upper * 8 * SPAN:(upper + 1) * 8 * SPAN]
+            send(block, block, pass_send.at[batch], pass_recv.at[batch], in_plane(0, 0, 1 - c))
 
     pass_on(group(near), 0)
     pass_on(group(far), 1)
@@ -289,7 +300,7 @@
             pltpu.VMEM((Z, 16, LANES), jnp.bfloat16),
             pltpu.VMEM((Z, ROWS, LANES), jnp.float32),
             pltpu.VMEM((FSDP, 3, ROWS, LANES), jnp.float32),
-            dma((4,)), pltpu.SemaphoreType.REGULAR((3,)), dma, dma, dma, dma, dma, dma((3,)), dma((3,)), dma((3,)), dma((3,)), dma((3,)),
+            dma((4,)), pltpu.SemaphoreType.REGULAR((3,)), dma, dma, dma, dma, dma, dma((3,)), dma((3,)), dma((6,)), dma((3,)), dma((3,)),
         ],
         compiler_params=pltpu.CompilerParams(collective_id=0, has_side_effects=True, vmem_limit_bytes=60 * 1024 * 1024),
         name="outer_step",

time: 36.8 us -> 36.7 us (level)
  no operation moved by 1% of the time
where the time goes in v7:
time: 36.7 us; the launch traced here: 36.5 us
  Pallas kernels  35.9 us (98%)
  between operations  0.64 us (2%)
    pallas_call x1, Pallas kernels, step(): pl.pallas_call(kernel, out_shape=(pltpu.VMEM((ROWS, COLS), jnp.float32),...  34.8 us
    pallas_call x1, Pallas kernels, step(): pl.pallas_call(finish, out_shape=(jax.ShapeDtypeStruct((ROWS, COLS), jnp....  1.03 us

profile of v7, /device:TPU:1, one launch (start us, length us, event | category | flops | bytes accessed | tf_op | source)
XLA Modules:
  0.0 36.5 jit_solution(16660596658002986042)
XLA Ops:
  0.6 34.8 %outer_step.1 = (f32[8,6144]{1,0:T(8,128)S(1)}, f32[8,6144]{1,0:T(8,128)S(1)}, bf16[80,6144]{1,0:T(8,128)(2,1)S(1)}) custom-call(bf16[1,8,6144]{2,1,0:T(8,128)(2,1)} %local_hbm.1, f32[8,6144]{1,0:T(8,128)} %base_hbm.1, f32[8,6144]{1,0:T(8,128)} %moment_hbm.1, s32[1,8,48]{2,1,0:T(8,128)} %codes_hbm.1), custom_call_target="tpu_custom_call" | custom-call | tf_op jit(solution)/shard_map/outer_step/pallas_call | solution.py:280
  35.5 1.0 %write_out.1 = (f32[8,6144]{1,0:T(8,128)}, f32[8,6144]{1,0:T(8,128)}, bf16[64,6144]{1,0:T(8,128)(2,1)}) custom-call(f32[8,6144]{1,0:T(8,128)S(1)} %get-tuple-element.6.new_base, f32[8,6144]{1,0:T(8,128)S(1)} %get-tuple-element.7.new_moment, bf16[80,6144]{1,0:T(8,128)(2,1)S(1)} %get-tuple-element.8.rows), custom_call_target="tpu_custom_call" | custom-call | tf_op jit(solution)/shard_map/write_out/pallas_call | solution.py:308
